TPU v7x, 32 devices: a whole 2x2x4 slice. The times are simulated.
32 devices in a mesh: grp: 2 (over x), row: 16 (over z, y, core).
Axes of the slice: x: 2, y: 2, z: 4, core: 2. Of those that a mesh axis runs over, the one named last changes fastest.
Arguments:
- sources: bfloat16 [32, 8, 8, 1024], P(('grp', 'row')), parts along dimension 0, may hold values from -6 to 6
- far_left: bfloat16 [64, 15, 48, 1024], P(('grp', 'row')), parts along dimension 0, may hold values from -0.1875 to 0.1875
- far_right: bfloat16 [64, 15, 48, 1024], P(('grp', 'row')), parts along dimension 0, may hold values from -0.078125 to 0.078125
- ranks: int32 [64, 15], P(('grp', 'row')), parts along dimension 0, may hold values from 16 to 48
- near_blocks: bfloat16 [6, 1024, 1024], P('grp'), parts along dimension 0, may hold values from -0.1875 to 0.1875
- near_offsets: int32 [6, 2], P('grp'), parts along dimension 0, may hold values from -1 to 1, as said below
Outputs:
- fields: float32 [32, 8, 8, 1024], P(('grp', 'row')), parts along dimension 0
There are 2 independent parts, one for each index of `grp`. A program takes and returns all parts, laid end to end along the dimension named above; each array names one. Nothing has to cross between parts.
Inputs may be any that keep to these rules, and one draw needn't show every extreme that they name: `near_offsets`: the rows are 3 distinct offsets (a, b); row 0 is the self offset (0, 0).
All inputs are finite; a program needn't handle non-finite values.
Results may differ from a plain program's by a relative error of at most 0.0014.
Values may be sent and summed in bfloat16 or wider, within the bound.
A program may use at most 64 MiB of HBM per device.

v0:
```python
import jax
import jax.numpy as jnp
from jax import lax
from jax.sharding import PartitionSpec as P

RANK = 48
ECOL = 8
SLOTS = 15


def from_behind(value, axis, by):
    count = lax.axis_size(axis)
    return lax.ppermute(value, axis, [(i, (i + by) % count) for i in range(count)])


def padded_2(block, sides, width):
    for axis, dim in sides:
        count = lax.axis_size(axis)
        forward = [(i, i + 1) for i in range(count - 1)]
        backward = [(target, source) for source, target in forward]
        low = lax.ppermute(
            lax.slice_in_dim(block, block.shape[dim] - width, None, axis=dim), axis, forward
        )
        high = lax.ppermute(lax.slice_in_dim(block, 0, width, axis=dim), axis, backward)
        block = jnp.concatenate([low, block, high], axis=dim)
    return block


def slot_mask(rank_row, row_offset, near_offsets):
    col_offset = jnp.arange(SLOTS, dtype=jnp.int32) - (ECOL - 1)
    hit = jnp.any(
        (near_offsets[:, 0][:, None] == row_offset)
        & (near_offsets[:, 1][:, None] == col_offset[None, :]),
        axis=0,
    )
    live = jnp.arange(RANK, dtype=jnp.int32)[None, :] < rank_row[:, None]
    return (live & jnp.logical_not(hit)[:, None]).astype(jnp.float32)


def spread(coeffs):
    padded = jnp.pad(coeffs, ((ECOL, ECOL), (0, 0), (0, 0), (0, 0)))
    columns = [padded[2 * ECOL - 1 - k : 3 * ECOL - 1 - k, k, :, :] for k in range(SLOTS)]
    return jnp.stack(columns, axis=1)


def far_term(source_row, left, right, keep):
    coeffs = jnp.einsum("sbn,krn->skbr", source_row, left, preferred_element_type=jnp.float32)
    coeffs = (coeffs * keep[None, :, None, :]).astype(jnp.bfloat16)
    return jnp.einsum("jkbr,krn->jbn", spread(coeffs), right, preferred_element_type=jnp.float32)


def local(sources, far_left, far_right, ranks, near_blocks, near_offsets):
    cycle_size = lax.axis_size("row")
    place = lax.axis_index("row")
    keep_all = jnp.stack(
        [slot_mask(ranks[w], place - cycle_size * w, near_offsets) for w in range(2)], axis=0
    )
    ecol, beams, width = (sources.shape[1], sources.shape[2], sources.shape[3])

    def source_term(source_row, source_index):
        wrap_bit = (source_index + place >= cycle_size).astype(jnp.int32)
        left = lax.dynamic_index_in_dim(far_left, wrap_bit, 0, keepdims=False)
        right = lax.dynamic_index_in_dim(far_right, wrap_bit, 0, keepdims=False)
        keep = lax.dynamic_index_in_dim(keep_all, wrap_bit, 0, keepdims=False)
        return far_term(source_row, left, right, keep)

    gathered = lax.all_gather(sources, "row", axis=0, tiled=True)

    def step(source_index, accums):
        down_acc, up_acc = accums
        source_row = lax.dynamic_index_in_dim(gathered, source_index, 0, keepdims=False)
        down_acc = down_acc + source_term(source_row, source_index)
        down_acc = from_behind(down_acc, "row", -1)
        return (down_acc, up_acc)

    start = (jnp.zeros((ecol, beams, width), jnp.float32), jnp.zeros((1,), jnp.float32))
    far, unused_up = lax.fori_loop(0, cycle_size, step, start)
    beside = padded_2(sources, (("row", 0),), 1)
    beside = jnp.pad(beside, ((0, 0), (1, 1), (0, 0), (0, 0)))
    near = jnp.zeros((ecol * beams, width), jnp.float32)
    for index in range(near_blocks.shape[0]):
        row_offset = near_offsets[index, 0]
        col_offset = near_offsets[index, 1]
        anchor = (1 - row_offset, 1 - col_offset, jnp.int32(0), jnp.int32(0))
        shifted = lax.dynamic_slice(beside, anchor, (1, ecol, beams, width))
        near = near + jnp.dot(
            shifted.reshape(-1, width), near_blocks[index], preferred_element_type=jnp.float32
        )
    return (near.reshape(ecol, beams, width) + far).reshape(1, ecol, beams, width)


def solution(mesh):
    placed = (
        P(("grp", "row"), None, None, None),
        P(("grp", "row"), None, None, None),
        P(("grp", "row"), None, None, None),
        P(("grp", "row"), None),
        P("grp", None, None),
        P("grp", None),
    )
    return jax.shard_map(
        local,
        mesh=mesh,
        in_specs=placed,
        out_specs=P(("grp", "row"), None, None, None),
        check_vma=False,
    )
```

profile of v0, /device:TPU:0, one launch (start us, length us, event | category | flops | bytes accessed | tf_op | source)
XLA Modules:
  0.0 249.0 jit_solution(835424933795626141)
XLA Ops:
  29.0 24.7 %all-gather.2.cloned.1.call-done = bf16[16,8,8,1024]{3,2,1,0:T(8,128)(2,1)} async-done(((bf16[1,8,8,1024]{3,2,1,0:T(8,128)(2,1)}), bf16[16,8,8,1024]{3,2,1,0:T(8,128)(2,1)}) %all-gather.2.cloned.1.call-update) | async-done | bytes 2097168 | tf_op jit(solution)/shard_map/all_gather | solution.py:67
  53.7 185.6 %while.15 = (s32[]{:T(128)}, f32[8,8,1024]{2,1,0:T(8,128)S(1)}, s32[]{:T(128)}, bf16[2,15,48,1024]{3,2,1,0:T(8,128)(2,1)}, bf16[16,8,8,1024]{3,2,1,0:T(8,128)(2,...) while((s32[]{:T(128)}, f32[8,8,1024]{2,1,0:T(8,128)S(1)}, ...), condition=%wide.region_3.4_spmd, body=%wide.region_2.3_spmd.sunk | while | flops 188901376 | bytes 8549533 | solution.py:77
  59.0 3.9 %collective-permute-done = f32[8,8,1024]{2,1,0:T(8,128)S(1)} collective-permute-done((f32[8,8,1024]{2,1,0:T(8,128)S(1)}, f32[8,8,1024]{2,1,0:T(8,128)S(1)}, u32[]{:S(2)}, u32[]{:S(2)}) %collective-permute-start) | collective-permute-done | bytes 262176 | tf_op jit(solution)/shard_map/while/body/eval_jaxpr/ppermute | solution.py:13
  66.1 4.7 %collective-permute-start = (f32[8,8,1024]{2,1,0:T(8,128)S(1)}, f32[8,8,1024]{2,1,0:T(8,128)S(1)}, u32[]{:S(2)}, u32[]{:S(2)}) collective-permute-start(f32[8,8,1024]{2,1,0:T(8,128)S(1)} %fusion.81), channel_id=1, source_target_pairs={{0,15},{1,0},{2,1},{3,2},{4,3},{5,4},{6,5},{7,6},{8,7},{9,8},{10,9... | collective-permute-start | bytes 786440 | tf_op jit(solution)/shard_map/while/body/eval_jaxpr/ppermute | solution.py:13
  70.7 3.9 %collective-permute-done = f32[8,8,1024]{2,1,0:T(8,128)S(1)} collective-permute-done((f32[8,8,1024]{2,1,0:T(8,128)S(1)}, f32[8,8,1024]{2,1,0:T(8,128)S(1)}, u32[]{:S(2)}, u32[]{:S(2)}) %collective-permute-start) | collective-permute-done | bytes 262176 | tf_op jit(solution)/shard_map/while/body/eval_jaxpr/ppermute | solution.py:13
  77.8 4.7 %collective-permute-start = (f32[8,8,1024]{2,1,0:T(8,128)S(1)}, f32[8,8,1024]{2,1,0:T(8,128)S(1)}, u32[]{:S(2)}, u32[]{:S(2)}) collective-permute-start(f32[8,8,1024]{2,1,0:T(8,128)S(1)} %fusion.81), channel_id=1, source_target_pairs={{0,15},{1,0},{2,1},{3,2},{4,3},{5,4},{6,5},{7,6},{8,7},{9,8},{10,9... | collective-permute-start | bytes 786440 | tf_op jit(solution)/shard_map/while/body/eval_jaxpr/ppermute | solution.py:13
  82.5 3.9 %collective-permute-done = f32[8,8,1024]{2,1,0:T(8,128)S(1)} collective-permute-done((f32[8,8,1024]{2,1,0:T(8,128)S(1)}, f32[8,8,1024]{2,1,0:T(8,128)S(1)}, u32[]{:S(2)}, u32[]{:S(2)}) %collective-permute-start) | collective-permute-done | bytes 262176 | tf_op jit(solution)/shard_map/while/body/eval_jaxpr/ppermute | solution.py:13
  89.6 4.7 %collective-permute-start = (f32[8,8,1024]{2,1,0:T(8,128)S(1)}, f32[8,8,1024]{2,1,0:T(8,128)S(1)}, u32[]{:S(2)}, u32[]{:S(2)}) collective-permute-start(f32[8,8,1024]{2,1,0:T(8,128)S(1)} %fusion.81), channel_id=1, source_target_pairs={{0,15},{1,0},{2,1},{3,2},{4,3},{5,4},{6,5},{7,6},{8,7},{9,8},{10,9... | collective-permute-start | bytes 786440 | tf_op jit(solution)/shard_map/while/body/eval_jaxpr/ppermute | solution.py:13
  94.2 3.9 %collective-permute-done = f32[8,8,1024]{2,1,0:T(8,128)S(1)} collective-permute-done((f32[8,8,1024]{2,1,0:T(8,128)S(1)}, f32[8,8,1024]{2,1,0:T(8,128)S(1)}, u32[]{:S(2)}, u32[]{:S(2)}) %collective-permute-start) | collective-permute-done | bytes 262176 | tf_op jit(solution)/shard_map/while/body/eval_jaxpr/ppermute | solution.py:13
  101.4 4.7 %collective-permute-start = (f32[8,8,1024]{2,1,0:T(8,128)S(1)}, f32[8,8,1024]{2,1,0:T(8,128)S(1)}, u32[]{:S(2)}, u32[]{:S(2)}) collective-permute-start(f32[8,8,1024]{2,1,0:T(8,128)S(1)} %fusion.81), channel_id=1, source_target_pairs={{0,15},{1,0},{2,1},{3,2},{4,3},{5,4},{6,5},{7,6},{8,7},{9,8},{10,9... | collective-permute-start | bytes 786440 | tf_op jit(solution)/shard_map/while/body/eval_jaxpr/ppermute | solution.py:13
  106.0 3.9 %collective-permute-done = f32[8,8,1024]{2,1,0:T(8,128)S(1)} collective-permute-done((f32[8,8,1024]{2,1,0:T(8,128)S(1)}, f32[8,8,1024]{2,1,0:T(8,128)S(1)}, u32[]{:S(2)}, u32[]{:S(2)}) %collective-permute-start) | collective-permute-done | bytes 262176 | tf_op jit(solution)/shard_map/while/body/eval_jaxpr/ppermute | solution.py:13
  113.1 4.7 %collective-permute-start = (f32[8,8,1024]{2,1,0:T(8,128)S(1)}, f32[8,8,1024]{2,1,0:T(8,128)S(1)}, u32[]{:S(2)}, u32[]{:S(2)}) collective-permute-start(f32[8,8,1024]{2,1,0:T(8,128)S(1)} %fusion.81), channel_id=1, source_target_pairs={{0,15},{1,0},{2,1},{3,2},{4,3},{5,4},{6,5},{7,6},{8,7},{9,8},{10,9... | collective-permute-start | bytes 786440 | tf_op jit(solution)/shard_map/while/body/eval_jaxpr/ppermute | solution.py:13
  117.8 3.9 %collective-permute-done = f32[8,8,1024]{2,1,0:T(8,128)S(1)} collective-permute-done((f32[8,8,1024]{2,1,0:T(8,128)S(1)}, f32[8,8,1024]{2,1,0:T(8,128)S(1)}, u32[]{:S(2)}, u32[]{:S(2)}) %collective-permute-start) | collective-permute-done | bytes 262176 | tf_op jit(solution)/shard_map/while/body/eval_jaxpr/ppermute | solution.py:13
  124.9 4.7 %collective-permute-start = (f32[8,8,1024]{2,1,0:T(8,128)S(1)}, f32[8,8,1024]{2,1,0:T(8,128)S(1)}, u32[]{:S(2)}, u32[]{:S(2)}) collective-permute-start(f32[8,8,1024]{2,1,0:T(8,128)S(1)} %fusion.81), channel_id=1, source_target_pairs={{0,15},{1,0},{2,1},{3,2},{4,3},{5,4},{6,5},{7,6},{8,7},{9,8},{10,9... | collective-permute-start | bytes 786440 | tf_op jit(solution)/shard_map/while/body/eval_jaxpr/ppermute | solution.py:13
  129.5 3.9 %collective-permute-done = f32[8,8,1024]{2,1,0:T(8,128)S(1)} collective-permute-done((f32[8,8,1024]{2,1,0:T(8,128)S(1)}, f32[8,8,1024]{2,1,0:T(8,128)S(1)}, u32[]{:S(2)}, u32[]{:S(2)}) %collective-permute-start) | collective-permute-done | bytes 262176 | tf_op jit(solution)/shard_map/while/body/eval_jaxpr/ppermute | solution.py:13
  136.6 4.7 %collective-permute-start = (f32[8,8,1024]{2,1,0:T(8,128)S(1)}, f32[8,8,1024]{2,1,0:T(8,128)S(1)}, u32[]{:S(2)}, u32[]{:S(2)}) collective-permute-start(f32[8,8,1024]{2,1,0:T(8,128)S(1)} %fusion.81), channel_id=1, source_target_pairs={{0,15},{1,0},{2,1},{3,2},{4,3},{5,4},{6,5},{7,6},{8,7},{9,8},{10,9... | collective-permute-start | bytes 786440 | tf_op jit(solution)/shard_map/while/body/eval_jaxpr/ppermute | solution.py:13
  141.3 3.9 %collective-permute-done = f32[8,8,1024]{2,1,0:T(8,128)S(1)} collective-permute-done((f32[8,8,1024]{2,1,0:T(8,128)S(1)}, f32[8,8,1024]{2,1,0:T(8,128)S(1)}, u32[]{:S(2)}, u32[]{:S(2)}) %collective-permute-start) | collective-permute-done | bytes 262176 | tf_op jit(solution)/shard_map/while/body/eval_jaxpr/ppermute | solution.py:13
  148.4 4.7 %collective-permute-start = (f32[8,8,1024]{2,1,0:T(8,128)S(1)}, f32[8,8,1024]{2,1,0:T(8,128)S(1)}, u32[]{:S(2)}, u32[]{:S(2)}) collective-permute-start(f32[8,8,1024]{2,1,0:T(8,128)S(1)} %fusion.81), channel_id=1, source_target_pairs={{0,15},{1,0},{2,1},{3,2},{4,3},{5,4},{6,5},{7,6},{8,7},{9,8},{10,9... | collective-permute-start | bytes 786440 | tf_op jit(solution)/shard_map/while/body/eval_jaxpr/ppermute | solution.py:13
  153.1 3.9 %collective-permute-done = f32[8,8,1024]{2,1,0:T(8,128)S(1)} collective-permute-done((f32[8,8,1024]{2,1,0:T(8,128)S(1)}, f32[8,8,1024]{2,1,0:T(8,128)S(1)}, u32[]{:S(2)}, u32[]{:S(2)}) %collective-permute-start) | collective-permute-done | bytes 262176 | tf_op jit(solution)/shard_map/while/body/eval_jaxpr/ppermute | solution.py:13
  160.2 4.7 %collective-permute-start = (f32[8,8,1024]{2,1,0:T(8,128)S(1)}, f32[8,8,1024]{2,1,0:T(8,128)S(1)}, u32[]{:S(2)}, u32[]{:S(2)}) collective-permute-start(f32[8,8,1024]{2,1,0:T(8,128)S(1)} %fusion.81), channel_id=1, source_target_pairs={{0,15},{1,0},{2,1},{3,2},{4,3},{5,4},{6,5},{7,6},{8,7},{9,8},{10,9... | collective-permute-start | bytes 786440 | tf_op jit(solution)/shard_map/while/body/eval_jaxpr/ppermute | solution.py:13
  164.8 3.9 %collective-permute-done = f32[8,8,1024]{2,1,0:T(8,128)S(1)} collective-permute-done((f32[8,8,1024]{2,1,0:T(8,128)S(1)}, f32[8,8,1024]{2,1,0:T(8,128)S(1)}, u32[]{:S(2)}, u32[]{:S(2)}) %collective-permute-start) | collective-permute-done | bytes 262176 | tf_op jit(solution)/shard_map/while/body/eval_jaxpr/ppermute | solution.py:13
  171.9 4.7 %collective-permute-start = (f32[8,8,1024]{2,1,0:T(8,128)S(1)}, f32[8,8,1024]{2,1,0:T(8,128)S(1)}, u32[]{:S(2)}, u32[]{:S(2)}) collective-permute-start(f32[8,8,1024]{2,1,0:T(8,128)S(1)} %fusion.81), channel_id=1, source_target_pairs={{0,15},{1,0},{2,1},{3,2},{4,3},{5,4},{6,5},{7,6},{8,7},{9,8},{10,9... | collective-permute-start | bytes 786440 | tf_op jit(solution)/shard_map/while/body/eval_jaxpr/ppermute | solution.py:13
  176.6 3.9 %collective-permute-done = f32[8,8,1024]{2,1,0:T(8,128)S(1)} collective-permute-done((f32[8,8,1024]{2,1,0:T(8,128)S(1)}, f32[8,8,1024]{2,1,0:T(8,128)S(1)}, u32[]{:S(2)}, u32[]{:S(2)}) %collective-permute-start) | collective-permute-done | bytes 262176 | tf_op jit(solution)/shard_map/while/body/eval_jaxpr/ppermute | solution.py:13
  183.7 4.7 %collective-permute-start = (f32[8,8,1024]{2,1,0:T(8,128)S(1)}, f32[8,8,1024]{2,1,0:T(8,128)S(1)}, u32[]{:S(2)}, u32[]{:S(2)}) collective-permute-start(f32[8,8,1024]{2,1,0:T(8,128)S(1)} %fusion.81), channel_id=1, source_target_pairs={{0,15},{1,0},{2,1},{3,2},{4,3},{5,4},{6,5},{7,6},{8,7},{9,8},{10,9... | collective-permute-start | bytes 786440 | tf_op jit(solution)/shard_map/while/body/eval_jaxpr/ppermute | solution.py:13
  188.4 3.9 %collective-permute-done = f32[8,8,1024]{2,1,0:T(8,128)S(1)} collective-permute-done((f32[8,8,1024]{2,1,0:T(8,128)S(1)}, f32[8,8,1024]{2,1,0:T(8,128)S(1)}, u32[]{:S(2)}, u32[]{:S(2)}) %collective-permute-start) | collective-permute-done | bytes 262176 | tf_op jit(solution)/shard_map/while/body/eval_jaxpr/ppermute | solution.py:13
  195.5 4.7 %collective-permute-start = (f32[8,8,1024]{2,1,0:T(8,128)S(1)}, f32[8,8,1024]{2,1,0:T(8,128)S(1)}, u32[]{:S(2)}, u32[]{:S(2)}) collective-permute-start(f32[8,8,1024]{2,1,0:T(8,128)S(1)} %fusion.81), channel_id=1, source_target_pairs={{0,15},{1,0},{2,1},{3,2},{4,3},{5,4},{6,5},{7,6},{8,7},{9,8},{10,9... | collective-permute-start | bytes 786440 | tf_op jit(solution)/shard_map/while/body/eval_jaxpr/ppermute | solution.py:13
  200.1 3.9 %collective-permute-done = f32[8,8,1024]{2,1,0:T(8,128)S(1)} collective-permute-done((f32[8,8,1024]{2,1,0:T(8,128)S(1)}, f32[8,8,1024]{2,1,0:T(8,128)S(1)}, u32[]{:S(2)}, u32[]{:S(2)}) %collective-permute-start) | collective-permute-done | bytes 262176 | tf_op jit(solution)/shard_map/while/body/eval_jaxpr/ppermute | solution.py:13
  207.2 4.7 %collective-permute-start = (f32[8,8,1024]{2,1,0:T(8,128)S(1)}, f32[8,8,1024]{2,1,0:T(8,128)S(1)}, u32[]{:S(2)}, u32[]{:S(2)}) collective-permute-start(f32[8,8,1024]{2,1,0:T(8,128)S(1)} %fusion.81), channel_id=1, source_target_pairs={{0,15},{1,0},{2,1},{3,2},{4,3},{5,4},{6,5},{7,6},{8,7},{9,8},{10,9... | collective-permute-start | bytes 786440 | tf_op jit(solution)/shard_map/while/body/eval_jaxpr/ppermute | solution.py:13
  211.9 3.9 %collective-permute-done = f32[8,8,1024]{2,1,0:T(8,128)S(1)} collective-permute-done((f32[8,8,1024]{2,1,0:T(8,128)S(1)}, f32[8,8,1024]{2,1,0:T(8,128)S(1)}, u32[]{:S(2)}, u32[]{:S(2)}) %collective-permute-start) | collective-permute-done | bytes 262176 | tf_op jit(solution)/shard_map/while/body/eval_jaxpr/ppermute | solution.py:13
  219.0 4.7 %collective-permute-start = (f32[8,8,1024]{2,1,0:T(8,128)S(1)}, f32[8,8,1024]{2,1,0:T(8,128)S(1)}, u32[]{:S(2)}, u32[]{:S(2)}) collective-permute-start(f32[8,8,1024]{2,1,0:T(8,128)S(1)} %fusion.81), channel_id=1, source_target_pairs={{0,15},{1,0},{2,1},{3,2},{4,3},{5,4},{6,5},{7,6},{8,7},{9,8},{10,9... | collective-permute-start | bytes 786440 | tf_op jit(solution)/shard_map/while/body/eval_jaxpr/ppermute | solution.py:13
  223.7 3.9 %collective-permute-done = f32[8,8,1024]{2,1,0:T(8,128)S(1)} collective-permute-done((f32[8,8,1024]{2,1,0:T(8,128)S(1)}, f32[8,8,1024]{2,1,0:T(8,128)S(1)}, u32[]{:S(2)}, u32[]{:S(2)}) %collective-permute-start) | collective-permute-done | bytes 262176 | tf_op jit(solution)/shard_map/while/body/eval_jaxpr/ppermute | solution.py:13
  230.8 4.7 %collective-permute-start = (f32[8,8,1024]{2,1,0:T(8,128)S(1)}, f32[8,8,1024]{2,1,0:T(8,128)S(1)}, u32[]{:S(2)}, u32[]{:S(2)}) collective-permute-start(f32[8,8,1024]{2,1,0:T(8,128)S(1)} %fusion.81), channel_id=1, source_target_pairs={{0,15},{1,0},{2,1},{3,2},{4,3},{5,4},{6,5},{7,6},{8,7},{9,8},{10,9... | collective-permute-start | bytes 786440 | tf_op jit(solution)/shard_map/while/body/eval_jaxpr/ppermute | solution.py:13
  (315 shorter events, 74.2 us)
Async XLA Ops:
  6.5 47.1 %all-gather.2.cloned.1.call-start = ((), (), s32[]{:S(2)}) async-start(), calls=%async_computation | async-start | bytes 2228224 | tf_op jit(solution)/shard_map/all_gather | solution.py:67
  7.3 14.9 %collective-permute-start.1 = (bf16[1,8,8,1024]{3,2,1,0:T(8,128)(2,1)}, bf16[1,8,8,1024]{3,2,1,0:T(8,128)(2,1)S(1)}, u32[]{:S(2)}, u32[]{:S(2)}) collective-permute-start(bf16[1,8,8,1024]{3,2,1,0:T(8,128)(2,1)} %param.8), channel_id=1, source_target_pairs={{0,1},{1,2},{2,3},{3,4},{4,5},{5,6},{6,7},{7,8},{8,9},{9,10},{10,1... | collective-permute-start | bytes 393224 | tf_op jit(solution)/shard_map/ppermute | solution.py:21
  9.6 12.5 %collective-permute-start.2 = (bf16[1,8,8,1024]{3,2,1,0:T(8,128)(2,1)}, bf16[1,8,8,1024]{3,2,1,0:T(8,128)(2,1)S(1)}, u32[]{:S(2)}, u32[]{:S(2)}) collective-permute-start(bf16[1,8,8,1024]{3,2,1,0:T(8,128)(2,1)} %param.8), channel_id=1, source_target_pairs={{1,0},{2,1},{3,2},{4,3},{5,4},{6,5},{7,6},{8,7},{9,8},{10,9},{11,1... | collective-permute-start | bytes 393224 | tf_op jit(solution)/shard_map/ppermute | solution.py:24
  22.1 31.6 %copy-start = (bf16[2,15,48,1024]{3,2,1,0:T(8,128)(2,1)S(1)}, bf16[2,15,48,1024]{3,2,1,0:T(8,128)(2,1)}, u32[]{:S(2)}) copy-start(bf16[2,15,48,1024]{3,2,1,0:T(8,128)(2,1)} %param.10) | copy-start | bytes 8847364
  23.3 3.0 %copy-start.1 = (bf16[3,10,8,1024]{3,2,1,0:T(8,128)(2,1)}, bf16[3,10,8,1024]{3,2,1,0:T(8,128)(2,1)S(1)}, u32[]{:S(2)}) copy-start(bf16[3,10,8,1024]{3,2,1,0:T(8,128)(2,1)S(1)} %fusion.54) | copy-start | bytes 1474564
  57.0 5.9 %collective-permute-start = (f32[8,8,1024]{2,1,0:T(8,128)S(1)}, f32[8,8,1024]{2,1,0:T(8,128)S(1)}, u32[]{:S(2)}, u32[]{:S(2)}) collective-permute-start(f32[8,8,1024]{2,1,0:T(8,128)S(1)} %fusion.81), channel_id=1, source_target_pairs={{0,15},{1,0},{2,1},{3,2},{4,3},{5,4},{6,5},{7,6},{8,7},{9,8},{10,9... | collective-permute-start | bytes 786440 | tf_op jit(solution)/shard_map/while/body/eval_jaxpr/ppermute | solution.py:13
  66.1 8.5 %collective-permute-start = (f32[8,8,1024]{2,1,0:T(8,128)S(1)}, f32[8,8,1024]{2,1,0:T(8,128)S(1)}, u32[]{:S(2)}, u32[]{:S(2)}) collective-permute-start(f32[8,8,1024]{2,1,0:T(8,128)S(1)} %fusion.81), channel_id=1, source_target_pairs={{0,15},{1,0},{2,1},{3,2},{4,3},{5,4},{6,5},{7,6},{8,7},{9,8},{10,9... | collective-permute-start | bytes 786440 | tf_op jit(solution)/shard_map/while/body/eval_jaxpr/ppermute | solution.py:13
  77.8 8.5 %collective-permute-start = (f32[8,8,1024]{2,1,0:T(8,128)S(1)}, f32[8,8,1024]{2,1,0:T(8,128)S(1)}, u32[]{:S(2)}, u32[]{:S(2)}) collective-permute-start(f32[8,8,1024]{2,1,0:T(8,128)S(1)} %fusion.81), channel_id=1, source_target_pairs={{0,15},{1,0},{2,1},{3,2},{4,3},{5,4},{6,5},{7,6},{8,7},{9,8},{10,9... | collective-permute-start | bytes 786440 | tf_op jit(solution)/shard_map/while/body/eval_jaxpr/ppermute | solution.py:13
  89.6 8.5 %collective-permute-start = (f32[8,8,1024]{2,1,0:T(8,128)S(1)}, f32[8,8,1024]{2,1,0:T(8,128)S(1)}, u32[]{:S(2)}, u32[]{:S(2)}) collective-permute-start(f32[8,8,1024]{2,1,0:T(8,128)S(1)} %fusion.81), channel_id=1, source_target_pairs={{0,15},{1,0},{2,1},{3,2},{4,3},{5,4},{6,5},{7,6},{8,7},{9,8},{10,9... | collective-permute-start | bytes 786440 | tf_op jit(solution)/shard_map/while/body/eval_jaxpr/ppermute | solution.py:13
  101.4 8.5 %collective-permute-start = (f32[8,8,1024]{2,1,0:T(8,128)S(1)}, f32[8,8,1024]{2,1,0:T(8,128)S(1)}, u32[]{:S(2)}, u32[]{:S(2)}) collective-permute-start(f32[8,8,1024]{2,1,0:T(8,128)S(1)} %fusion.81), channel_id=1, source_target_pairs={{0,15},{1,0},{2,1},{3,2},{4,3},{5,4},{6,5},{7,6},{8,7},{9,8},{10,9... | collective-permute-start | bytes 786440 | tf_op jit(solution)/shard_map/while/body/eval_jaxpr/ppermute | solution.py:13
  113.1 8.5 %collective-permute-start = (f32[8,8,1024]{2,1,0:T(8,128)S(1)}, f32[8,8,1024]{2,1,0:T(8,128)S(1)}, u32[]{:S(2)}, u32[]{:S(2)}) collective-permute-start(f32[8,8,1024]{2,1,0:T(8,128)S(1)} %fusion.81), channel_id=1, source_target_pairs={{0,15},{1,0},{2,1},{3,2},{4,3},{5,4},{6,5},{7,6},{8,7},{9,8},{10,9... | collective-permute-start | bytes 786440 | tf_op jit(solution)/shard_map/while/body/eval_jaxpr/ppermute | solution.py:13
  124.9 8.5 %collective-permute-start = (f32[8,8,1024]{2,1,0:T(8,128)S(1)}, f32[8,8,1024]{2,1,0:T(8,128)S(1)}, u32[]{:S(2)}, u32[]{:S(2)}) collective-permute-start(f32[8,8,1024]{2,1,0:T(8,128)S(1)} %fusion.81), channel_id=1, source_target_pairs={{0,15},{1,0},{2,1},{3,2},{4,3},{5,4},{6,5},{7,6},{8,7},{9,8},{10,9... | collective-permute-start | bytes 786440 | tf_op jit(solution)/shard_map/while/body/eval_jaxpr/ppermute | solution.py:13
  136.6 8.5 %collective-permute-start = (f32[8,8,1024]{2,1,0:T(8,128)S(1)}, f32[8,8,1024]{2,1,0:T(8,128)S(1)}, u32[]{:S(2)}, u32[]{:S(2)}) collective-permute-start(f32[8,8,1024]{2,1,0:T(8,128)S(1)} %fusion.81), channel_id=1, source_target_pairs={{0,15},{1,0},{2,1},{3,2},{4,3},{5,4},{6,5},{7,6},{8,7},{9,8},{10,9... | collective-permute-start | bytes 786440 | tf_op jit(solution)/shard_map/while/body/eval_jaxpr/ppermute | solution.py:13
  148.4 8.5 %collective-permute-start = (f32[8,8,1024]{2,1,0:T(8,128)S(1)}, f32[8,8,1024]{2,1,0:T(8,128)S(1)}, u32[]{:S(2)}, u32[]{:S(2)}) collective-permute-start(f32[8,8,1024]{2,1,0:T(8,128)S(1)} %fusion.81), channel_id=1, source_target_pairs={{0,15},{1,0},{2,1},{3,2},{4,3},{5,4},{6,5},{7,6},{8,7},{9,8},{10,9... | collective-permute-start | bytes 786440 | tf_op jit(solution)/shard_map/while/body/eval_jaxpr/ppermute | solution.py:13
  160.2 8.5 %collective-permute-start = (f32[8,8,1024]{2,1,0:T(8,128)S(1)}, f32[8,8,1024]{2,1,0:T(8,128)S(1)}, u32[]{:S(2)}, u32[]{:S(2)}) collective-permute-start(f32[8,8,1024]{2,1,0:T(8,128)S(1)} %fusion.81), channel_id=1, source_target_pairs={{0,15},{1,0},{2,1},{3,2},{4,3},{5,4},{6,5},{7,6},{8,7},{9,8},{10,9... | collective-permute-start | bytes 786440 | tf_op jit(solution)/shard_map/while/body/eval_jaxpr/ppermute | solution.py:13
  171.9 8.5 %collective-permute-start = (f32[8,8,1024]{2,1,0:T(8,128)S(1)}, f32[8,8,1024]{2,1,0:T(8,128)S(1)}, u32[]{:S(2)}, u32[]{:S(2)}) collective-permute-start(f32[8,8,1024]{2,1,0:T(8,128)S(1)} %fusion.81), channel_id=1, source_target_pairs={{0,15},{1,0},{2,1},{3,2},{4,3},{5,4},{6,5},{7,6},{8,7},{9,8},{10,9... | collective-permute-start | bytes 786440 | tf_op jit(solution)/shard_map/while/body/eval_jaxpr/ppermute | solution.py:13
  183.7 8.5 %collective-permute-start = (f32[8,8,1024]{2,1,0:T(8,128)S(1)}, f32[8,8,1024]{2,1,0:T(8,128)S(1)}, u32[]{:S(2)}, u32[]{:S(2)}) collective-permute-start(f32[8,8,1024]{2,1,0:T(8,128)S(1)} %fusion.81), channel_id=1, source_target_pairs={{0,15},{1,0},{2,1},{3,2},{4,3},{5,4},{6,5},{7,6},{8,7},{9,8},{10,9... | collective-permute-start | bytes 786440 | tf_op jit(solution)/shard_map/while/body/eval_jaxpr/ppermute | solution.py:13
  195.5 8.5 %collective-permute-start = (f32[8,8,1024]{2,1,0:T(8,128)S(1)}, f32[8,8,1024]{2,1,0:T(8,128)S(1)}, u32[]{:S(2)}, u32[]{:S(2)}) collective-permute-start(f32[8,8,1024]{2,1,0:T(8,128)S(1)} %fusion.81), channel_id=1, source_target_pairs={{0,15},{1,0},{2,1},{3,2},{4,3},{5,4},{6,5},{7,6},{8,7},{9,8},{10,9... | collective-permute-start | bytes 786440 | tf_op jit(solution)/shard_map/while/body/eval_jaxpr/ppermute | solution.py:13
  207.2 8.5 %collective-permute-start = (f32[8,8,1024]{2,1,0:T(8,128)S(1)}, f32[8,8,1024]{2,1,0:T(8,128)S(1)}, u32[]{:S(2)}, u32[]{:S(2)}) collective-permute-start(f32[8,8,1024]{2,1,0:T(8,128)S(1)} %fusion.81), channel_id=1, source_target_pairs={{0,15},{1,0},{2,1},{3,2},{4,3},{5,4},{6,5},{7,6},{8,7},{9,8},{10,9... | collective-permute-start | bytes 786440 | tf_op jit(solution)/shard_map/while/body/eval_jaxpr/ppermute | solution.py:13
  219.0 8.5 %collective-permute-start = (f32[8,8,1024]{2,1,0:T(8,128)S(1)}, f32[8,8,1024]{2,1,0:T(8,128)S(1)}, u32[]{:S(2)}, u32[]{:S(2)}) collective-permute-start(f32[8,8,1024]{2,1,0:T(8,128)S(1)} %fusion.81), channel_id=1, source_target_pairs={{0,15},{1,0},{2,1},{3,2},{4,3},{5,4},{6,5},{7,6},{8,7},{9,8},{10,9... | collective-permute-start | bytes 786440 | tf_op jit(solution)/shard_map/while/body/eval_jaxpr/ppermute | solution.py:13
  230.8 8.5 %collective-permute-start = (f32[8,8,1024]{2,1,0:T(8,128)S(1)}, f32[8,8,1024]{2,1,0:T(8,128)S(1)}, u32[]{:S(2)}, u32[]{:S(2)}) collective-permute-start(f32[8,8,1024]{2,1,0:T(8,128)S(1)} %fusion.81), channel_id=1, source_target_pairs={{0,15},{1,0},{2,1},{3,2},{4,3},{5,4},{6,5},{7,6},{8,7},{9,8},{10,9... | collective-permute-start | bytes 786440 | tf_op jit(solution)/shard_map/while/body/eval_jaxpr/ppermute | solution.py:13
Sparse Core Ops, SparseCore 0:
  9.5 44.1 all-gather.1
where the time goes:
time: 250 us; the launch traced here: 249 us
  waiting for transfers between devices  87.6 us (35%)
  starting transfers between devices  75.5 us (30%)
  matrix products  55.8 us (22%)
  between operations  20.8 us (8%)
  local copies, waits for them, and re-layouts  6.14 us (2%)
    ppermute x16, starting transfers between devices, from_behind(): lax.ppermute(value, axis, [(i, (i + by) % count) for i in range(count)])  71.9 us
    ppermute x16, waiting for transfers between devices, from_behind(): lax.ppermute(value, axis, [(i, (i + by) % count) for i in range(count)])  62.2 us
    dot_general x16, matrix products, far_term(): jnp.einsum('sbn,krn->skbr', source_row, left, preferred_element_type=jnp....  37.4 us
    all_gather x1, waiting for transfers between devices, local(): gathered = lax.all_gather(sources, 'row', axis=0, tiled=True)  24.7 us
    dot_general x16, matrix products, far_term(): jnp.einsum('jkbr,krn->jbn', spread(coeffs), right, preferred_element_type...  9.73 us
    dot_general x3, matrix products, local(): jnp.dot(shifted.reshape(-1, width), near_blocks[index], preferred_element...  8.65 us
  transfers between devices with their start and end apart: 19, of which 17 were waited for; matrix products, arithmetic and copies ran while one was open for 4% of the time, Pallas kernels for 0%

commit v1 on v0

--- a/solution.py
+++ b/solution.py
@@ -64,7 +64,13 @@
         keep = lax.dynamic_index_in_dim(keep_all, wrap_bit, 0, keepdims=False)
         return far_term(source_row, left, right, keep)
 
-    gathered = lax.all_gather(sources, "row", axis=0, tiled=True)
+    devices = lax.axis_size("row")
+    moving, parts = (sources, [sources])
+    for _ in range(devices - 1):
+        moving = lax.ppermute(moving, "row", [(i_2, (i_2 + 1) % devices) for i_2 in range(devices)])
+        parts.insert(0, moving)
+    merged = jnp.concatenate(parts, axis=0)
+    gathered = jnp.roll(merged, (lax.axis_index("row") + 1) * sources.shape[0], axis=0)
 
     def step(source_index, accums):
         down_acc, up_acc = accums

time: 250 us -> 309 us (1.24)
  waiting for transfers between devices: 87.6 us -> 151 us
  between operations: 20.8 us -> 7.86 us
  local copies, waits for them, and re-layouts: 6.14 us -> 16.4 us
    ppermute x0 -> x15, waiting for transfers between devices: none -> 89.2 us  [local(): lax.ppermute(moving, 'row', [(i_2, (i_2 + 1) % devices) for i_2 in range(...]
    all_gather x1 -> x0, waiting for transfers between devices: 24.7 us -> none  [local(): gathered = lax.all_gather(sources, 'row', axis=0, tiled=True)]
    unnamed x4 -> x55, local copies, waits for them, and re-layouts: 0.01 us -> 8.68 us
  transfers between devices with their start and end apart: 19 -> 33, of which waited for: 17 -> 30; matrix products, arithmetic and copies ran while one was open for 4% -> 3% of each run, Pallas kernels for 0% -> 0%
where the time goes in v1:
time: 309 us; the launch traced here: 308 us
  waiting for transfers between devices  151 us (49%)
  starting transfers between devices  73.2 us (24%)
  matrix products  55.8 us (18%)
  local copies, waits for them, and re-layouts  16.4 us (5%)
  between operations  7.86 us (3%)
    ppermute x15, waiting for transfers between devices, local(): lax.ppermute(moving, 'row', [(i_2, (i_2 + 1) % devices) for i_2 in range(...  89.2 us
    ppermute x16, starting transfers between devices, from_behind(): lax.ppermute(value, axis, [(i, (i + by) % count) for i in range(count)])  70 us
    ppermute x16, waiting for transfers between devices, from_behind(): lax.ppermute(value, axis, [(i, (i + by) % count) for i in range(count)])  62.2 us
    dot_general x16, matrix products, far_term(): jnp.einsum('sbn,krn->skbr', source_row, left, preferred_element_type=jnp....  37.4 us
    dot_general x16, matrix products, far_term(): jnp.einsum('jkbr,krn->jbn', spread(coeffs), right, preferred_element_type...  9.75 us
    unnamed x55, local copies, waits for them, and re-layouts  8.68 us
    dot_general x3, matrix products, local(): jnp.dot(shifted.reshape(-1, width), near_blocks[index], preferred_element...  8.67 us
  transfers between devices with their start and end apart: 33, of which 30 were waited for; matrix products, arithmetic and copies ran while one was open for 3% of the time, Pallas kernels for 0%

profile of v1, /device:TPU:0, one launch (start us, length us, event | category | flops | bytes accessed | tf_op | source)
XLA Modules:
  0.0 307.8 jit_solution(6548240284721276752)
XLA Ops:
  0.5 7.9 %collective-permute-done.3 = bf16[1,8,8,1024]{3,2,1,0:T(8,128)(2,1)S(1)} collective-permute-done((bf16[1,8,8,1024]{3,2,1,0:T(8,128)(2,1)}, bf16[1,8,8,1024]{3,2,1,0:T(8,128)(2,1)S(1)}, u32[]{:S(2)}, u32[]{:S(2)}) %collective-permute-start.3) | collective-permute-done | bytes 131104 | tf_op jit(solution)/shard_map/ppermute | solution.py:70
  8.3 7.1 %collective-permute-done.4 = bf16[1,8,8,1024]{3,2,1,0:T(8,128)(2,1)S(1)} collective-permute-done((bf16[1,8,8,1024]{3,2,1,0:T(8,128)(2,1)S(1)}, bf16[1,8,8,1024]{3,2,1,0:T(8,128)(2,1)S(1)}, u32[]{:S(2)}, u32[]{:S(2)}) %collective-permute-start.4) | collective-permute-done | bytes 131104 | tf_op jit(solution)/shard_map/ppermute | solution.py:70
  15.4 7.1 %collective-permute-done.5 = bf16[1,8,8,1024]{3,2,1,0:T(8,128)(2,1)S(1)} collective-permute-done((bf16[1,8,8,1024]{3,2,1,0:T(8,128)(2,1)S(1)}, bf16[1,8,8,1024]{3,2,1,0:T(8,128)(2,1)S(1)}, u32[]{:S(2)}, u32[]{:S(2)}) %collective-permute-start.5) | collective-permute-done | bytes 131104 | tf_op jit(solution)/shard_map/ppermute | solution.py:70
  22.5 7.1 %collective-permute-done.6 = bf16[1,8,8,1024]{3,2,1,0:T(8,128)(2,1)S(1)} collective-permute-done((bf16[1,8,8,1024]{3,2,1,0:T(8,128)(2,1)S(1)}, bf16[1,8,8,1024]{3,2,1,0:T(8,128)(2,1)S(1)}, u32[]{:S(2)}, u32[]{:S(2)}) %collective-permute-start.6) | collective-permute-done | bytes 131104 | tf_op jit(solution)/shard_map/ppermute | solution.py:70
  29.6 7.1 %collective-permute-done.7 = bf16[1,8,8,1024]{3,2,1,0:T(8,128)(2,1)S(1)} collective-permute-done((bf16[1,8,8,1024]{3,2,1,0:T(8,128)(2,1)S(1)}, bf16[1,8,8,1024]{3,2,1,0:T(8,128)(2,1)S(1)}, u32[]{:S(2)}, u32[]{:S(2)}) %collective-permute-start.7) | collective-permute-done | bytes 131104 | tf_op jit(solution)/shard_map/ppermute | solution.py:70
  36.7 7.1 %collective-permute-done.8 = bf16[1,8,8,1024]{3,2,1,0:T(8,128)(2,1)S(1)} collective-permute-done((bf16[1,8,8,1024]{3,2,1,0:T(8,128)(2,1)S(1)}, bf16[1,8,8,1024]{3,2,1,0:T(8,128)(2,1)S(1)}, u32[]{:S(2)}, u32[]{:S(2)}) %collective-permute-start.8) | collective-permute-done | bytes 131104 | tf_op jit(solution)/shard_map/ppermute | solution.py:70
  46.4 4.5 %collective-permute-done.9 = bf16[1,8,8,1024]{3,2,1,0:T(8,128)(2,1)S(1)} collective-permute-done((bf16[1,8,8,1024]{3,2,1,0:T(8,128)(2,1)S(1)}, bf16[1,8,8,1024]{3,2,1,0:T(8,128)(2,1)S(1)}, u32[]{:S(2)}, u32[]{:S(2)}) %collective-permute-start.9) | collective-permute-done | bytes 131104 | tf_op jit(solution)/shard_map/ppermute | solution.py:70
  51.6 6.4 %collective-permute-done.10 = bf16[1,8,8,1024]{3,2,1,0:T(8,128)(2,1)S(1)} collective-permute-done((bf16[1,8,8,1024]{3,2,1,0:T(8,128)(2,1)S(1)}, bf16[1,8,8,1024]{3,2,1,0:T(8,128)(2,1)S(1)}, u32[]{:S(2)}, u32[]{:S(2)}) %collective-permute-start.10) | collective-permute-done | bytes 131104 | tf_op jit(solution)/shard_map/ppermute | solution.py:70
  58.6 6.4 %collective-permute-done.11 = bf16[1,8,8,1024]{3,2,1,0:T(8,128)(2,1)S(1)} collective-permute-done((bf16[1,8,8,1024]{3,2,1,0:T(8,128)(2,1)S(1)}, bf16[1,8,8,1024]{3,2,1,0:T(8,128)(2,1)S(1)}, u32[]{:S(2)}, u32[]{:S(2)}) %collective-permute-start.11) | collective-permute-done | bytes 131104 | tf_op jit(solution)/shard_map/ppermute | solution.py:70
  65.2 7.0 %collective-permute-done.12 = bf16[1,8,8,1024]{3,2,1,0:T(8,128)(2,1)S(1)} collective-permute-done((bf16[1,8,8,1024]{3,2,1,0:T(8,128)(2,1)S(1)}, bf16[1,8,8,1024]{3,2,1,0:T(8,128)(2,1)S(1)}, u32[]{:S(2)}, u32[]{:S(2)}) %collective-permute-start.12) | collective-permute-done | bytes 131104 | tf_op jit(solution)/shard_map/ppermute | solution.py:70
  72.9 6.3 %collective-permute-done.13 = bf16[1,8,8,1024]{3,2,1,0:T(8,128)(2,1)S(1)} collective-permute-done((bf16[1,8,8,1024]{3,2,1,0:T(8,128)(2,1)S(1)}, bf16[1,8,8,1024]{3,2,1,0:T(8,128)(2,1)S(1)}, u32[]{:S(2)}, u32[]{:S(2)}) %collective-permute-start.13) | collective-permute-done | bytes 131104 | tf_op jit(solution)/shard_map/ppermute | solution.py:70
  79.3 7.0 %collective-permute-done.14 = bf16[1,8,8,1024]{3,2,1,0:T(8,128)(2,1)S(1)} collective-permute-done((bf16[1,8,8,1024]{3,2,1,0:T(8,128)(2,1)S(1)}, bf16[1,8,8,1024]{3,2,1,0:T(8,128)(2,1)S(1)}, u32[]{:S(2)}, u32[]{:S(2)}) %collective-permute-start.14) | collective-permute-done | bytes 131104 | tf_op jit(solution)/shard_map/ppermute | solution.py:70
  99.4 4.1 %collective-permute-done.16 = bf16[1,8,8,1024]{3,2,1,0:T(8,128)(2,1)S(1)} collective-permute-done((bf16[1,8,8,1024]{3,2,1,0:T(8,128)(2,1)S(1)}, bf16[1,8,8,1024]{3,2,1,0:T(8,128)(2,1)S(1)}, u32[]{:S(2)}, u32[]{:S(2)}) %collective-permute-start.16) | collective-permute-done | bytes 131104 | tf_op jit(solution)/shard_map/ppermute | solution.py:70
  106.3 4.3 %collective-permute-done.17 = bf16[1,8,8,1024]{3,2,1,0:T(8,128)(2,1)S(1)} collective-permute-done((bf16[1,8,8,1024]{3,2,1,0:T(8,128)(2,1)S(1)}, bf16[1,8,8,1024]{3,2,1,0:T(8,128)(2,1)S(1)}, u32[]{:S(2)}, u32[]{:S(2)}) %collective-permute-start.17) | collective-permute-done | bytes 131104 | tf_op jit(solution)/shard_map/ppermute | solution.py:70
  121.1 183.8 %while.15 = (s32[]{:T(128)}, f32[8,8,1024]{2,1,0:T(8,128)S(1)}, s32[]{:T(128)}, bf16[2,15,48,1024]{3,2,1,0:T(8,128)(2,1)}, bf16[16,8,8,1024]{3,2,1,0:T(8,128)(2,...) while((s32[]{:T(128)}, f32[8,8,1024]{2,1,0:T(8,128)S(1)}, ...), condition=%wide.region_3.4_spmd, body=%wide.region_2.3_spmd.sunk | while | flops 188901376 | bytes 8549533 | solution.py:83
  131.7 4.7 %collective-permute-start = (f32[8,8,1024]{2,1,0:T(8,128)S(1)}, f32[8,8,1024]{2,1,0:T(8,128)S(1)}, u32[]{:S(2)}, u32[]{:S(2)}) collective-permute-start(f32[8,8,1024]{2,1,0:T(8,128)S(1)} %fusion.81), channel_id=1, source_target_pairs={{0,15},{1,0},{2,1},{3,2},{4,3},{5,4},{6,5},{7,6},{8,7},{9,8},{10,9... | collective-permute-start | bytes 786440 | tf_op jit(solution)/shard_map/while/body/eval_jaxpr/ppermute | solution.py:13
  136.3 3.9 %collective-permute-done = f32[8,8,1024]{2,1,0:T(8,128)S(1)} collective-permute-done((f32[8,8,1024]{2,1,0:T(8,128)S(1)}, f32[8,8,1024]{2,1,0:T(8,128)S(1)}, u32[]{:S(2)}, u32[]{:S(2)}) %collective-permute-start) | collective-permute-done | bytes 262176 | tf_op jit(solution)/shard_map/while/body/eval_jaxpr/ppermute | solution.py:13
  143.4 4.7 %collective-permute-start = (f32[8,8,1024]{2,1,0:T(8,128)S(1)}, f32[8,8,1024]{2,1,0:T(8,128)S(1)}, u32[]{:S(2)}, u32[]{:S(2)}) collective-permute-start(f32[8,8,1024]{2,1,0:T(8,128)S(1)} %fusion.81), channel_id=1, source_target_pairs={{0,15},{1,0},{2,1},{3,2},{4,3},{5,4},{6,5},{7,6},{8,7},{9,8},{10,9... | collective-permute-start | bytes 786440 | tf_op jit(solution)/shard_map/while/body/eval_jaxpr/ppermute | solution.py:13
  155.2 4.7 %collective-permute-start = (f32[8,8,1024]{2,1,0:T(8,128)S(1)}, f32[8,8,1024]{2,1,0:T(8,128)S(1)}, u32[]{:S(2)}, u32[]{:S(2)}) collective-permute-start(f32[8,8,1024]{2,1,0:T(8,128)S(1)} %fusion.81), channel_id=1, source_target_pairs={{0,15},{1,0},{2,1},{3,2},{4,3},{5,4},{6,5},{7,6},{8,7},{9,8},{10,9... | collective-permute-start | bytes 786440 | tf_op jit(solution)/shard_map/while/body/eval_jaxpr/ppermute | solution.py:13
  159.8 3.9 %collective-permute-done = f32[8,8,1024]{2,1,0:T(8,128)S(1)} collective-permute-done((f32[8,8,1024]{2,1,0:T(8,128)S(1)}, f32[8,8,1024]{2,1,0:T(8,128)S(1)}, u32[]{:S(2)}, u32[]{:S(2)}) %collective-permute-start) | collective-permute-done | bytes 262176 | tf_op jit(solution)/shard_map/while/body/eval_jaxpr/ppermute | solution.py:13
  166.9 4.7 %collective-permute-start = (f32[8,8,1024]{2,1,0:T(8,128)S(1)}, f32[8,8,1024]{2,1,0:T(8,128)S(1)}, u32[]{:S(2)}, u32[]{:S(2)}) collective-permute-start(f32[8,8,1024]{2,1,0:T(8,128)S(1)} %fusion.81), channel_id=1, source_target_pairs={{0,15},{1,0},{2,1},{3,2},{4,3},{5,4},{6,5},{7,6},{8,7},{9,8},{10,9... | collective-permute-start | bytes 786440 | tf_op jit(solution)/shard_map/while/body/eval_jaxpr/ppermute | solution.py:13
  178.7 4.7 %collective-permute-start = (f32[8,8,1024]{2,1,0:T(8,128)S(1)}, f32[8,8,1024]{2,1,0:T(8,128)S(1)}, u32[]{:S(2)}, u32[]{:S(2)}) collective-permute-start(f32[8,8,1024]{2,1,0:T(8,128)S(1)} %fusion.81), channel_id=1, source_target_pairs={{0,15},{1,0},{2,1},{3,2},{4,3},{5,4},{6,5},{7,6},{8,7},{9,8},{10,9... | collective-permute-start | bytes 786440 | tf_op jit(solution)/shard_map/while/body/eval_jaxpr/ppermute | solution.py:13
  190.5 4.7 %collective-permute-start = (f32[8,8,1024]{2,1,0:T(8,128)S(1)}, f32[8,8,1024]{2,1,0:T(8,128)S(1)}, u32[]{:S(2)}, u32[]{:S(2)}) collective-permute-start(f32[8,8,1024]{2,1,0:T(8,128)S(1)} %fusion.81), channel_id=1, source_target_pairs={{0,15},{1,0},{2,1},{3,2},{4,3},{5,4},{6,5},{7,6},{8,7},{9,8},{10,9... | collective-permute-start | bytes 786440 | tf_op jit(solution)/shard_map/while/body/eval_jaxpr/ppermute | solution.py:13
  202.2 4.7 %collective-permute-start = (f32[8,8,1024]{2,1,0:T(8,128)S(1)}, f32[8,8,1024]{2,1,0:T(8,128)S(1)}, u32[]{:S(2)}, u32[]{:S(2)}) collective-permute-start(f32[8,8,1024]{2,1,0:T(8,128)S(1)} %fusion.81), channel_id=1, source_target_pairs={{0,15},{1,0},{2,1},{3,2},{4,3},{5,4},{6,5},{7,6},{8,7},{9,8},{10,9... | collective-permute-start | bytes 786440 | tf_op jit(solution)/shard_map/while/body/eval_jaxpr/ppermute | solution.py:13
  214.0 4.7 %collective-permute-start = (f32[8,8,1024]{2,1,0:T(8,128)S(1)}, f32[8,8,1024]{2,1,0:T(8,128)S(1)}, u32[]{:S(2)}, u32[]{:S(2)}) collective-permute-start(f32[8,8,1024]{2,1,0:T(8,128)S(1)} %fusion.81), channel_id=1, source_target_pairs={{0,15},{1,0},{2,1},{3,2},{4,3},{5,4},{6,5},{7,6},{8,7},{9,8},{10,9... | collective-permute-start | bytes 786440 | tf_op jit(solution)/shard_map/while/body/eval_jaxpr/ppermute | solution.py:13
  225.8 4.7 %collective-permute-start = (f32[8,8,1024]{2,1,0:T(8,128)S(1)}, f32[8,8,1024]{2,1,0:T(8,128)S(1)}, u32[]{:S(2)}, u32[]{:S(2)}) collective-permute-start(f32[8,8,1024]{2,1,0:T(8,128)S(1)} %fusion.81), channel_id=1, source_target_pairs={{0,15},{1,0},{2,1},{3,2},{4,3},{5,4},{6,5},{7,6},{8,7},{9,8},{10,9... | collective-permute-start | bytes 786440 | tf_op jit(solution)/shard_map/while/body/eval_jaxpr/ppermute | solution.py:13
  237.5 4.7 %collective-permute-start = (f32[8,8,1024]{2,1,0:T(8,128)S(1)}, f32[8,8,1024]{2,1,0:T(8,128)S(1)}, u32[]{:S(2)}, u32[]{:S(2)}) collective-permute-start(f32[8,8,1024]{2,1,0:T(8,128)S(1)} %fusion.81), channel_id=1, source_target_pairs={{0,15},{1,0},{2,1},{3,2},{4,3},{5,4},{6,5},{7,6},{8,7},{9,8},{10,9... | collective-permute-start | bytes 786440 | tf_op jit(solution)/shard_map/while/body/eval_jaxpr/ppermute | solution.py:13
  249.3 4.7 %collective-permute-start = (f32[8,8,1024]{2,1,0:T(8,128)S(1)}, f32[8,8,1024]{2,1,0:T(8,128)S(1)}, u32[]{:S(2)}, u32[]{:S(2)}) collective-permute-start(f32[8,8,1024]{2,1,0:T(8,128)S(1)} %fusion.81), channel_id=1, source_target_pairs={{0,15},{1,0},{2,1},{3,2},{4,3},{5,4},{6,5},{7,6},{8,7},{9,8},{10,9... | collective-permute-start | bytes 786440 | tf_op jit(solution)/shard_map/while/body/eval_jaxpr/ppermute | solution.py:13
  261.1 4.7 %collective-permute-start = (f32[8,8,1024]{2,1,0:T(8,128)S(1)}, f32[8,8,1024]{2,1,0:T(8,128)S(1)}, u32[]{:S(2)}, u32[]{:S(2)}) collective-permute-start(f32[8,8,1024]{2,1,0:T(8,128)S(1)} %fusion.81), channel_id=1, source_target_pairs={{0,15},{1,0},{2,1},{3,2},{4,3},{5,4},{6,5},{7,6},{8,7},{9,8},{10,9... | collective-permute-start | bytes 786440 | tf_op jit(solution)/shard_map/while/body/eval_jaxpr/ppermute | solution.py:13
  272.8 4.7 %collective-permute-start = (f32[8,8,1024]{2,1,0:T(8,128)S(1)}, f32[8,8,1024]{2,1,0:T(8,128)S(1)}, u32[]{:S(2)}, u32[]{:S(2)}) collective-permute-start(f32[8,8,1024]{2,1,0:T(8,128)S(1)} %fusion.81), channel_id=1, source_target_pairs={{0,15},{1,0},{2,1},{3,2},{4,3},{5,4},{6,5},{7,6},{8,7},{9,8},{10,9... | collective-permute-start | bytes 786440 | tf_op jit(solution)/shard_map/while/body/eval_jaxpr/ppermute | solution.py:13
  284.6 4.7 %collective-permute-start = (f32[8,8,1024]{2,1,0:T(8,128)S(1)}, f32[8,8,1024]{2,1,0:T(8,128)S(1)}, u32[]{:S(2)}, u32[]{:S(2)}) collective-permute-start(f32[8,8,1024]{2,1,0:T(8,128)S(1)} %fusion.81), channel_id=1, source_target_pairs={{0,15},{1,0},{2,1},{3,2},{4,3},{5,4},{6,5},{7,6},{8,7},{9,8},{10,9... | collective-permute-start | bytes 786440 | tf_op jit(solution)/shard_map/while/body/eval_jaxpr/ppermute | solution.py:13
  296.4 4.7 %collective-permute-start = (f32[8,8,1024]{2,1,0:T(8,128)S(1)}, f32[8,8,1024]{2,1,0:T(8,128)S(1)}, u32[]{:S(2)}, u32[]{:S(2)}) collective-permute-start(f32[8,8,1024]{2,1,0:T(8,128)S(1)} %fusion.81), channel_id=1, source_target_pairs={{0,15},{1,0},{2,1},{3,2},{4,3},{5,4},{6,5},{7,6},{8,7},{9,8},{10,9... | collective-permute-start | bytes 786440 | tf_op jit(solution)/shard_map/while/body/eval_jaxpr/ppermute | solution.py:13
  (395 shorter events, 131.8 us)
Async XLA Ops:
  0.0 8.3 %collective-permute-start.3 = (bf16[1,8,8,1024]{3,2,1,0:T(8,128)(2,1)}, bf16[1,8,8,1024]{3,2,1,0:T(8,128)(2,1)S(1)}, u32[]{:S(2)}, u32[]{:S(2)}) collective-permute-start(bf16[1,8,8,1024]{3,2,1,0:T(8,128)(2,1)} %param.8), channel_id=1, source_target_pairs={{0,1},{1,2},{2,3},{3,4},{4,5},{5,6},{6,7},{7,8},{8,9},{9,10},{10,1... | collective-permute-start | bytes 393224 | tf_op jit(solution)/shard_map/ppermute | solution.py:70
  8.3 7.1 %collective-permute-start.4 = (bf16[1,8,8,1024]{3,2,1,0:T(8,128)(2,1)S(1)}, bf16[1,8,8,1024]{3,2,1,0:T(8,128)(2,1)S(1)}, u32[]{:S(2)}, u32[]{:S(2)}) collective-permute-start(bf16[1,8,8,1024]{3,2,1,0:T(8,128)(2,1)S(1)} %collective-permute-done.3), channel_id=1, source_target_pairs={{0,1},{1,2},{2,3},{3,4},{4,5},{5,6},{6,7},{7,8},{8,9},{9,10},{10,1... | collective-permute-start | bytes 393224 | tf_op jit(solution)/shard_map/ppermute | solution.py:70
  15.4 7.1 %collective-permute-start.5 = (bf16[1,8,8,1024]{3,2,1,0:T(8,128)(2,1)S(1)}, bf16[1,8,8,1024]{3,2,1,0:T(8,128)(2,1)S(1)}, u32[]{:S(2)}, u32[]{:S(2)}) collective-permute-start(bf16[1,8,8,1024]{3,2,1,0:T(8,128)(2,1)S(1)} %collective-permute-done.4), channel_id=1, source_target_pairs={{0,1},{1,2},{2,3},{3,4},{4,5},{5,6},{6,7},{7,8},{8,9},{9,10},{10,1... | collective-permute-start | bytes 393224 | tf_op jit(solution)/shard_map/ppermute | solution.py:70
  22.5 7.1 %collective-permute-start.6 = (bf16[1,8,8,1024]{3,2,1,0:T(8,128)(2,1)S(1)}, bf16[1,8,8,1024]{3,2,1,0:T(8,128)(2,1)S(1)}, u32[]{:S(2)}, u32[]{:S(2)}) collective-permute-start(bf16[1,8,8,1024]{3,2,1,0:T(8,128)(2,1)S(1)} %collective-permute-done.5), channel_id=1, source_target_pairs={{0,1},{1,2},{2,3},{3,4},{4,5},{5,6},{6,7},{7,8},{8,9},{9,10},{10,1... | collective-permute-start | bytes 393224 | tf_op jit(solution)/shard_map/ppermute | solution.py:70
  29.6 7.1 %collective-permute-start.7 = (bf16[1,8,8,1024]{3,2,1,0:T(8,128)(2,1)S(1)}, bf16[1,8,8,1024]{3,2,1,0:T(8,128)(2,1)S(1)}, u32[]{:S(2)}, u32[]{:S(2)}) collective-permute-start(bf16[1,8,8,1024]{3,2,1,0:T(8,128)(2,1)S(1)} %collective-permute-done.6), channel_id=1, source_target_pairs={{0,1},{1,2},{2,3},{3,4},{4,5},{5,6},{6,7},{7,8},{8,9},{9,10},{10,1... | collective-permute-start | bytes 393224 | tf_op jit(solution)/shard_map/ppermute | solution.py:70
  36.7 7.1 %collective-permute-start.8 = (bf16[1,8,8,1024]{3,2,1,0:T(8,128)(2,1)S(1)}, bf16[1,8,8,1024]{3,2,1,0:T(8,128)(2,1)S(1)}, u32[]{:S(2)}, u32[]{:S(2)}) collective-permute-start(bf16[1,8,8,1024]{3,2,1,0:T(8,128)(2,1)S(1)} %collective-permute-done.7), channel_id=1, source_target_pairs={{0,1},{1,2},{2,3},{3,4},{4,5},{5,6},{6,7},{7,8},{8,9},{9,10},{10,1... | collective-permute-start | bytes 393224 | tf_op jit(solution)/shard_map/ppermute | solution.py:70
  43.8 7.1 %collective-permute-start.9 = (bf16[1,8,8,1024]{3,2,1,0:T(8,128)(2,1)S(1)}, bf16[1,8,8,1024]{3,2,1,0:T(8,128)(2,1)S(1)}, u32[]{:S(2)}, u32[]{:S(2)}) collective-permute-start(bf16[1,8,8,1024]{3,2,1,0:T(8,128)(2,1)S(1)} %collective-permute-done.8), channel_id=1, source_target_pairs={{0,1},{1,2},{2,3},{3,4},{4,5},{5,6},{6,7},{7,8},{8,9},{9,10},{10,1... | collective-permute-start | bytes 393224 | tf_op jit(solution)/shard_map/ppermute | solution.py:70
  43.8 51.5 %collective-permute-start.1 = (bf16[1,8,8,1024]{3,2,1,0:T(8,128)(2,1)}, bf16[1,8,8,1024]{3,2,1,0:T(8,128)(2,1)S(1)}, u32[]{:S(2)}, u32[]{:S(2)}) collective-permute-start(bf16[1,8,8,1024]{3,2,1,0:T(8,128)(2,1)} %param.8), channel_id=1, source_target_pairs={{0,1},{1,2},{2,3},{3,4},{4,5},{5,6},{6,7},{7,8},{8,9},{9,10},{10,1... | collective-permute-start | bytes 393224 | tf_op jit(solution)/shard_map/ppermute | solution.py:21
  45.1 50.3 %collective-permute-start.2 = (bf16[1,8,8,1024]{3,2,1,0:T(8,128)(2,1)}, bf16[1,8,8,1024]{3,2,1,0:T(8,128)(2,1)S(1)}, u32[]{:S(2)}, u32[]{:S(2)}) collective-permute-start(bf16[1,8,8,1024]{3,2,1,0:T(8,128)(2,1)} %param.8), channel_id=1, source_target_pairs={{1,0},{2,1},{3,2},{4,3},{5,4},{6,5},{7,6},{8,7},{9,8},{10,9},{11,1... | collective-permute-start | bytes 393224 | tf_op jit(solution)/shard_map/ppermute | solution.py:24
  50.9 7.1 %collective-permute-start.10 = (bf16[1,8,8,1024]{3,2,1,0:T(8,128)(2,1)S(1)}, bf16[1,8,8,1024]{3,2,1,0:T(8,128)(2,1)S(1)}, u32[]{:S(2)}, u32[]{:S(2)}) collective-permute-start(bf16[1,8,8,1024]{3,2,1,0:T(8,128)(2,1)S(1)} %collective-permute-done.9), channel_id=1, source_target_pairs={{0,1},{1,2},{2,3},{3,4},{4,5},{5,6},{6,7},{7,8},{8,9},{9,10},{10,1... | collective-permute-start | bytes 393224 | tf_op jit(solution)/shard_map/ppermute | solution.py:70
  57.9 7.1 %collective-permute-start.11 = (bf16[1,8,8,1024]{3,2,1,0:T(8,128)(2,1)S(1)}, bf16[1,8,8,1024]{3,2,1,0:T(8,128)(2,1)S(1)}, u32[]{:S(2)}, u32[]{:S(2)}) collective-permute-start(bf16[1,8,8,1024]{3,2,1,0:T(8,128)(2,1)S(1)} %collective-permute-done.10), channel_id=1, source_target_pairs={{0,1},{1,2},{2,3},{3,4},{4,5},{5,6},{6,7},{7,8},{8,9},{9,10},{10,1... | collective-permute-start | bytes 393224 | tf_op jit(solution)/shard_map/ppermute | solution.py:70
  65.0 7.1 %collective-permute-start.12 = (bf16[1,8,8,1024]{3,2,1,0:T(8,128)(2,1)S(1)}, bf16[1,8,8,1024]{3,2,1,0:T(8,128)(2,1)S(1)}, u32[]{:S(2)}, u32[]{:S(2)}) collective-permute-start(bf16[1,8,8,1024]{3,2,1,0:T(8,128)(2,1)S(1)} %collective-permute-done.11), channel_id=1, source_target_pairs={{0,1},{1,2},{2,3},{3,4},{4,5},{5,6},{6,7},{7,8},{8,9},{9,10},{10,1... | collective-permute-start | bytes 393224 | tf_op jit(solution)/shard_map/ppermute | solution.py:70
  72.1 7.1 %collective-permute-start.13 = (bf16[1,8,8,1024]{3,2,1,0:T(8,128)(2,1)S(1)}, bf16[1,8,8,1024]{3,2,1,0:T(8,128)(2,1)S(1)}, u32[]{:S(2)}, u32[]{:S(2)}) collective-permute-start(bf16[1,8,8,1024]{3,2,1,0:T(8,128)(2,1)S(1)} %collective-permute-done.12), channel_id=1, source_target_pairs={{0,1},{1,2},{2,3},{3,4},{4,5},{5,6},{6,7},{7,8},{8,9},{9,10},{10,1... | collective-permute-start | bytes 393224 | tf_op jit(solution)/shard_map/ppermute | solution.py:70
  79.2 7.1 %collective-permute-start.14 = (bf16[1,8,8,1024]{3,2,1,0:T(8,128)(2,1)S(1)}, bf16[1,8,8,1024]{3,2,1,0:T(8,128)(2,1)S(1)}, u32[]{:S(2)}, u32[]{:S(2)}) collective-permute-start(bf16[1,8,8,1024]{3,2,1,0:T(8,128)(2,1)S(1)} %collective-permute-done.13), channel_id=1, source_target_pairs={{0,1},{1,2},{2,3},{3,4},{4,5},{5,6},{6,7},{7,8},{8,9},{9,10},{10,1... | collective-permute-start | bytes 393224 | tf_op jit(solution)/shard_map/ppermute | solution.py:70
  86.3 10.0 %collective-permute-start.15 = (bf16[1,8,8,1024]{3,2,1,0:T(8,128)(2,1)S(1)}, bf16[1,8,8,1024]{3,2,1,0:T(8,128)(2,1)S(1)}, u32[]{:S(2)}, u32[]{:S(2)}) collective-permute-start(bf16[1,8,8,1024]{3,2,1,0:T(8,128)(2,1)S(1)} %collective-permute-done.14), channel_id=1, source_target_pairs={{0,1},{1,2},{2,3},{3,4},{4,5},{5,6},{6,7},{7,8},{8,9},{9,10},{10,1... | collective-permute-start | bytes 393224 | tf_op jit(solution)/shard_map/ppermute | solution.py:70
  96.3 7.1 %collective-permute-start.16 = (bf16[1,8,8,1024]{3,2,1,0:T(8,128)(2,1)S(1)}, bf16[1,8,8,1024]{3,2,1,0:T(8,128)(2,1)S(1)}, u32[]{:S(2)}, u32[]{:S(2)}) collective-permute-start(bf16[1,8,8,1024]{3,2,1,0:T(8,128)(2,1)S(1)} %collective-permute-done.15), channel_id=1, source_target_pairs={{0,1},{1,2},{2,3},{3,4},{4,5},{5,6},{6,7},{7,8},{8,9},{9,10},{10,1... | collective-permute-start | bytes 393224 | tf_op jit(solution)/shard_map/ppermute | solution.py:70
  103.5 7.1 %collective-permute-start.17 = (bf16[1,8,8,1024]{3,2,1,0:T(8,128)(2,1)S(1)}, bf16[1,8,8,1024]{3,2,1,0:T(8,128)(2,1)S(1)}, u32[]{:S(2)}, u32[]{:S(2)}) collective-permute-start(bf16[1,8,8,1024]{3,2,1,0:T(8,128)(2,1)S(1)} %collective-permute-done.16), channel_id=1, source_target_pairs={{0,1},{1,2},{2,3},{3,4},{4,5},{5,6},{6,7},{7,8},{8,9},{9,10},{10,1... | collective-permute-start | bytes 393224 | tf_op jit(solution)/shard_map/ppermute | solution.py:70
  131.7 8.5 %collective-permute-start = (f32[8,8,1024]{2,1,0:T(8,128)S(1)}, f32[8,8,1024]{2,1,0:T(8,128)S(1)}, u32[]{:S(2)}, u32[]{:S(2)}) collective-permute-start(f32[8,8,1024]{2,1,0:T(8,128)S(1)} %fusion.81), channel_id=1, source_target_pairs={{0,15},{1,0},{2,1},{3,2},{4,3},{5,4},{6,5},{7,6},{8,7},{9,8},{10,9... | collective-permute-start | bytes 786440 | tf_op jit(solution)/shard_map/while/body/eval_jaxpr/ppermute | solution.py:13
  143.4 8.6 %collective-permute-start = (f32[8,8,1024]{2,1,0:T(8,128)S(1)}, f32[8,8,1024]{2,1,0:T(8,128)S(1)}, u32[]{:S(2)}, u32[]{:S(2)}) collective-permute-start(f32[8,8,1024]{2,1,0:T(8,128)S(1)} %fusion.81), channel_id=1, source_target_pairs={{0,15},{1,0},{2,1},{3,2},{4,3},{5,4},{6,5},{7,6},{8,7},{9,8},{10,9... | collective-permute-start | bytes 786440 | tf_op jit(solution)/shard_map/while/body/eval_jaxpr/ppermute | solution.py:13
  155.2 8.5 %collective-permute-start = (f32[8,8,1024]{2,1,0:T(8,128)S(1)}, f32[8,8,1024]{2,1,0:T(8,128)S(1)}, u32[]{:S(2)}, u32[]{:S(2)}) collective-permute-start(f32[8,8,1024]{2,1,0:T(8,128)S(1)} %fusion.81), channel_id=1, source_target_pairs={{0,15},{1,0},{2,1},{3,2},{4,3},{5,4},{6,5},{7,6},{8,7},{9,8},{10,9... | collective-permute-start | bytes 786440 | tf_op jit(solution)/shard_map/while/body/eval_jaxpr/ppermute | solution.py:13
  166.9 8.6 %collective-permute-start = (f32[8,8,1024]{2,1,0:T(8,128)S(1)}, f32[8,8,1024]{2,1,0:T(8,128)S(1)}, u32[]{:S(2)}, u32[]{:S(2)}) collective-permute-start(f32[8,8,1024]{2,1,0:T(8,128)S(1)} %fusion.81), channel_id=1, source_target_pairs={{0,15},{1,0},{2,1},{3,2},{4,3},{5,4},{6,5},{7,6},{8,7},{9,8},{10,9... | collective-permute-start | bytes 786440 | tf_op jit(solution)/shard_map/while/body/eval_jaxpr/ppermute | solution.py:13
  178.7 8.5 %collective-permute-start = (f32[8,8,1024]{2,1,0:T(8,128)S(1)}, f32[8,8,1024]{2,1,0:T(8,128)S(1)}, u32[]{:S(2)}, u32[]{:S(2)}) collective-permute-start(f32[8,8,1024]{2,1,0:T(8,128)S(1)} %fusion.81), channel_id=1, source_target_pairs={{0,15},{1,0},{2,1},{3,2},{4,3},{5,4},{6,5},{7,6},{8,7},{9,8},{10,9... | collective-permute-start | bytes 786440 | tf_op jit(solution)/shard_map/while/body/eval_jaxpr/ppermute | solution.py:13
  190.5 8.6 %collective-permute-start = (f32[8,8,1024]{2,1,0:T(8,128)S(1)}, f32[8,8,1024]{2,1,0:T(8,128)S(1)}, u32[]{:S(2)}, u32[]{:S(2)}) collective-permute-start(f32[8,8,1024]{2,1,0:T(8,128)S(1)} %fusion.81), channel_id=1, source_target_pairs={{0,15},{1,0},{2,1},{3,2},{4,3},{5,4},{6,5},{7,6},{8,7},{9,8},{10,9... | collective-permute-start | bytes 786440 | tf_op jit(solution)/shard_map/while/body/eval_jaxpr/ppermute | solution.py:13
  202.2 8.5 %collective-permute-start = (f32[8,8,1024]{2,1,0:T(8,128)S(1)}, f32[8,8,1024]{2,1,0:T(8,128)S(1)}, u32[]{:S(2)}, u32[]{:S(2)}) collective-permute-start(f32[8,8,1024]{2,1,0:T(8,128)S(1)} %fusion.81), channel_id=1, source_target_pairs={{0,15},{1,0},{2,1},{3,2},{4,3},{5,4},{6,5},{7,6},{8,7},{9,8},{10,9... | collective-permute-start | bytes 786440 | tf_op jit(solution)/shard_map/while/body/eval_jaxpr/ppermute | solution.py:13
  214.0 8.6 %collective-permute-start = (f32[8,8,1024]{2,1,0:T(8,128)S(1)}, f32[8,8,1024]{2,1,0:T(8,128)S(1)}, u32[]{:S(2)}, u32[]{:S(2)}) collective-permute-start(f32[8,8,1024]{2,1,0:T(8,128)S(1)} %fusion.81), channel_id=1, source_target_pairs={{0,15},{1,0},{2,1},{3,2},{4,3},{5,4},{6,5},{7,6},{8,7},{9,8},{10,9... | collective-permute-start | bytes 786440 | tf_op jit(solution)/shard_map/while/body/eval_jaxpr/ppermute | solution.py:13
  225.8 8.5 %collective-permute-start = (f32[8,8,1024]{2,1,0:T(8,128)S(1)}, f32[8,8,1024]{2,1,0:T(8,128)S(1)}, u32[]{:S(2)}, u32[]{:S(2)}) collective-permute-start(f32[8,8,1024]{2,1,0:T(8,128)S(1)} %fusion.81), channel_id=1, source_target_pairs={{0,15},{1,0},{2,1},{3,2},{4,3},{5,4},{6,5},{7,6},{8,7},{9,8},{10,9... | collective-permute-start | bytes 786440 | tf_op jit(solution)/shard_map/while/body/eval_jaxpr/ppermute | solution.py:13
  237.5 8.6 %collective-permute-start = (f32[8,8,1024]{2,1,0:T(8,128)S(1)}, f32[8,8,1024]{2,1,0:T(8,128)S(1)}, u32[]{:S(2)}, u32[]{:S(2)}) collective-permute-start(f32[8,8,1024]{2,1,0:T(8,128)S(1)} %fusion.81), channel_id=1, source_target_pairs={{0,15},{1,0},{2,1},{3,2},{4,3},{5,4},{6,5},{7,6},{8,7},{9,8},{10,9... | collective-permute-start | bytes 786440 | tf_op jit(solution)/shard_map/while/body/eval_jaxpr/ppermute | solution.py:13
  249.3 8.5 %collective-permute-start = (f32[8,8,1024]{2,1,0:T(8,128)S(1)}, f32[8,8,1024]{2,1,0:T(8,128)S(1)}, u32[]{:S(2)}, u32[]{:S(2)}) collective-permute-start(f32[8,8,1024]{2,1,0:T(8,128)S(1)} %fusion.81), channel_id=1, source_target_pairs={{0,15},{1,0},{2,1},{3,2},{4,3},{5,4},{6,5},{7,6},{8,7},{9,8},{10,9... | collective-permute-start | bytes 786440 | tf_op jit(solution)/shard_map/while/body/eval_jaxpr/ppermute | solution.py:13
  261.1 8.6 %collective-permute-start = (f32[8,8,1024]{2,1,0:T(8,128)S(1)}, f32[8,8,1024]{2,1,0:T(8,128)S(1)}, u32[]{:S(2)}, u32[]{:S(2)}) collective-permute-start(f32[8,8,1024]{2,1,0:T(8,128)S(1)} %fusion.81), channel_id=1, source_target_pairs={{0,15},{1,0},{2,1},{3,2},{4,3},{5,4},{6,5},{7,6},{8,7},{9,8},{10,9... | collective-permute-start | bytes 786440 | tf_op jit(solution)/shard_map/while/body/eval_jaxpr/ppermute | solution.py:13
  272.8 8.5 %collective-permute-start = (f32[8,8,1024]{2,1,0:T(8,128)S(1)}, f32[8,8,1024]{2,1,0:T(8,128)S(1)}, u32[]{:S(2)}, u32[]{:S(2)}) collective-permute-start(f32[8,8,1024]{2,1,0:T(8,128)S(1)} %fusion.81), channel_id=1, source_target_pairs={{0,15},{1,0},{2,1},{3,2},{4,3},{5,4},{6,5},{7,6},{8,7},{9,8},{10,9... | collective-permute-start | bytes 786440 | tf_op jit(solution)/shard_map/while/body/eval_jaxpr/ppermute | solution.py:13
  284.6 8.6 %collective-permute-start = (f32[8,8,1024]{2,1,0:T(8,128)S(1)}, f32[8,8,1024]{2,1,0:T(8,128)S(1)}, u32[]{:S(2)}, u32[]{:S(2)}) collective-permute-start(f32[8,8,1024]{2,1,0:T(8,128)S(1)} %fusion.81), channel_id=1, source_target_pairs={{0,15},{1,0},{2,1},{3,2},{4,3},{5,4},{6,5},{7,6},{8,7},{9,8},{10,9... | collective-permute-start | bytes 786440 | tf_op jit(solution)/shard_map/while/body/eval_jaxpr/ppermute | solution.py:13
  296.4 8.5 %collective-permute-start = (f32[8,8,1024]{2,1,0:T(8,128)S(1)}, f32[8,8,1024]{2,1,0:T(8,128)S(1)}, u32[]{:S(2)}, u32[]{:S(2)}) collective-permute-start(f32[8,8,1024]{2,1,0:T(8,128)S(1)} %fusion.81), channel_id=1, source_target_pairs={{0,15},{1,0},{2,1},{3,2},{4,3},{5,4},{6,5},{7,6},{8,7},{9,8},{10,9... | collective-permute-start | bytes 786440 | tf_op jit(solution)/shard_map/while/body/eval_jaxpr/ppermute | solution.py:13
  (13 other events, 452.4 us)
